TPU v7x, 32 devices: a whole 2x2x4 slice. The times are simulated.
32 devices in a mesh: groups: 1, dp: 1, tensor: 32 (over z, y, x, core).
Axes of the slice: x: 2, y: 2, z: 4, core: 2. Of those that a mesh axis runs over, the one named last changes fastest.
Arguments:
- queries: bfloat16 [128, 8192], P(('groups', 'dp'), 'tensor'), may hold values from -200 to 200
- cache: bfloat16 [32, 128, 128, 256], P('tensor', ('groups', 'dp')), may hold values from -6 to 6, as said below
- lengths: int32 [128], P(('groups', 'dp')), may hold values from 2 to 128, as said below
- request_adapter_index: int32 [128], P(('groups', 'dp')), may hold values from 0 to 7
- output_projection_weight: bfloat16 [8192, 8192], P('tensor'), may hold values from -0.125 to 0.125
- adapter_down_weight: bfloat16 [8, 8192, 64], P(('groups', 'dp'), 'tensor'), may hold values from -0.0625 to 0.0625
- adapter_up_weight: bfloat16 [8, 64, 8192], P(('groups', 'dp'), None, 'tensor'), may hold values from -0.75 to 0.75
Outputs:
- mixed: bfloat16 [8192, 128], P('tensor', ('groups', 'dp'))
Inputs may be any that keep to these rules, and one draw needn't show every extreme that they name: `lengths`: in each dp index's 128 requests at least one has length 128. `cache`: copies i and j are equal where i // 4 == j // 4.
All inputs are finite; a program needn't handle non-finite values.
Results may differ from a plain program's by a relative error of at most 0.006.
Values may be sent and summed in bfloat16 or wider, within the bound.
A program may use at most 64 MiB of HBM per device.

v0:
```python
import math

import jax
import jax.numpy as jnp
from jax import lax
from jax.sharding import PartitionSpec as P

HEAD = 128


def pick_terms(select, terms):
    return jnp.sum(jnp.where(select, terms, 0.0), axis=1)


def body(
    queries,
    cache,
    lengths,
    request_adapter_index,
    output_projection_weight,
    adapter_down_weight,
    adapter_up_weight,
):
    rows = queries.shape[0]
    width = queries.shape[1]
    heads = width // HEAD
    slots_count = cache.shape[2]
    keys_local = cache[0, :, :, :HEAD]
    values_local = cache[0, :, :, HEAD:]
    grouped = queries.reshape(rows, heads, HEAD)
    scores = jnp.einsum("rhe,rte->rht", grouped, keys_local, preferred_element_type=jnp.float32)
    scores = scores * (1.0 / math.sqrt(HEAD))
    live = jnp.arange(slots_count)[None, :] < lengths[:, None]
    scores = jnp.where(live[:, None, :], scores, jnp.float32(-1e30))
    top = jnp.max(scores, axis=-1, keepdims=True)
    expd = jnp.exp(scores - top)
    weights = (expd / jnp.sum(expd, axis=-1, keepdims=True)).astype(jnp.bfloat16)
    attended_state = jnp.einsum(
        "rht,rte->rhe", weights, values_local, preferred_element_type=jnp.float32
    )
    attended_state = attended_state.astype(jnp.bfloat16).reshape(rows, width)
    downs, ups = (
        lax.all_gather(adapter_down_weight, "dp", axis=0, tiled=True),
        lax.all_gather(adapter_up_weight, "dp", axis=0, tiled=True),
    )
    count = downs.shape[0]
    select = request_adapter_index[:, None] == jnp.arange(count)[None, :]
    parts = jnp.einsum("rd,adk->rak", attended_state, downs, preferred_element_type=jnp.float32)
    partial_low = pick_terms(select[:, :, None], parts)
    low_rank_state = lax.psum(partial_low, "tensor").astype(jnp.bfloat16)
    full = jnp.einsum("rk,akn->nar", low_rank_state, ups, preferred_element_type=jnp.float32)
    delta = pick_terms(jnp.transpose(select)[None, :, :], full)
    base = lax.psum_scatter(
        lax.dot_general(
            output_projection_weight,
            attended_state,
            (((0,), (1,)), ((), ())),
            preferred_element_type=jnp.float32,
        ),
        "tensor",
        scatter_dimension=0,
        tiled=True,
    )
    return (base + delta).astype(jnp.bfloat16)


def solution(mesh):
    return jax.shard_map(
        body,
        mesh=mesh,
        in_specs=(
            P(("groups", "dp"), "tensor"),
            P("tensor", ("groups", "dp"), None, None),
            P(("groups", "dp")),
            P(("groups", "dp")),
            P("tensor", None),
            P(("groups", "dp"), "tensor", None),
            P(("groups", "dp"), None, "tensor"),
        ),
        out_specs=P("tensor", ("groups", "dp")),
        check_vma=False,
    )
```

profile of v0, /device:TPU:0, one launch (start us, length us, event | category | flops | bytes accessed | tf_op | source)
XLA Modules:
  0.0 171.4 jit_solution(15766019691365541873)
XLA Ops:
  6.5 0.0 copy-start
  6.5 0.0 reduce-scatter.2.cloned.1.call-start
  6.5 0.9 reshape.65
  7.4 0.7 iota_compare_fusion
  8.2 4.6 %fusion.28 = (f32[128,2]{1,0:T(8,128)S(1)}, f32[128,2,128]{2,1,0:T(2,128)S(1)}) fusion(bf16[128,2,128]{2,1,0:T(2,128)(2,1)S(1)} %reshape.65, bf16[1,128,128,256]{3,2,1,0:T(8,128)(2,1)} %param.8, pred[128,128]{1,0:T(8,128)(4,1)S(1)} %iota_compare_fusion), kind=kOutput, calls=%fused_computation.30 | convolution fusion | flops 8519807 | bytes 4408320 | tf_op jit(solution)/shard_map/sub | solution.py:36
  12.8 0.0 copy-start.1
  12.8 3.6 %fusion.14 = bf16[128,2,128]{2,1,0:T(2,128)(2,1)S(1)} fusion(bf16[1,128,128,256]{3,2,1,0:T(8,128)(2,1)} %param.8, f32[128,2,128]{2,1,0:T(2,128)S(1)} %get-tuple-element.6, f32[128,2]{1,0:T(8,128)S(1)} %get-tuple-element.5), kind=kOutput, calls=%fused_computation.14 | convolution fusion | flops 8486912 | bytes 4391936 | tf_op jit(solution)/shard_map/rht,rte->rhe/dot_general | solution.py:38
  16.4 0.0 copy-done.1
  16.4 2.7 %convolution_bitcast_fusion = f32[8192,128]{0,1:T(8,128)} fusion(bf16[256,8192]{1,0:T(8,128)(2,1)S(1)} %copy-done.1, bf16[16,8,2,128]{3,2,1,0:T(2,128)(2,1)S(1)} %bitcast.41), kind=kOutput, calls=%fused_computation.1 | convolution fusion | flops 536870912 | bytes 8454144 | tf_op jit(solution)/shard_map/dot_general | solution.py:54
  19.1 0.0 copy-start.3
  19.1 0.0 copy-start.2
  19.1 0.0 reduce-scatter.2.cloned.1.call-update
  19.1 0.6 copy-done.3
  19.7 0.0 copy-done
  19.7 0.2 fusion.20
  20.0 42.3 %psum.7 = bf16[128,64]{0,1:T(8,128)(2,1)S(1)} all-reduce(f32[128,64]{0,1:T(8,128)S(1)} %select_reduce_fusion), channel_id=1, replica_groups=mesh['groups'=1,'dp'=1,'tensor'=32] {'tensor'}, use_global_device_ids=true, to_apply=%region_4.5 | all-reduce | flops 8192 | bytes 49152 | tf_op jit(solution)/shard_map/psum | solution.py:50
  62.3 0.0 copy-done.2
  62.3 0.3 fusion.8
  62.6 100.3 %reduce-scatter.2.cloned.1.call-done = f32[256,128]{0,1:T(8,128)} async-done(((f32[8192,128]{0,1:T(8,128)}), f32[256,128]{0,1:T(8,128)}) %reduce-scatter.2.cloned.1.call-update) | async-done | bytes 131088 | tf_op jit(solution)/shard_map/reduce_scatter | solution.py:53
  162.9 0.9 add_convert_fusion
  163.8 0.7 copy.9
  (3 shorter events, 0.0 us)
Async XLA Ops:
  6.5 13.2 %copy-start = (bf16[8,256,64]{1,2,0:T(8,128)(2,1)S(1)}, bf16[8,256,64]{1,2,0:T(8,128)(2,1)}, u32[]{:S(2)}) copy-start(bf16[8,256,64]{1,2,0:T(8,128)(2,1)} %param.12) | copy-start | bytes 786436
  6.5 156.3 %reduce-scatter.2.cloned.1.call-start = ((), (), s32[]{:S(2)}) async-start(), calls=%async_computation.1 | async-start | bytes 4325376 | tf_op jit(solution)/shard_map/reduce_scatter | solution.py:53
  12.8 3.6 %copy-start.1 = (bf16[256,8192]{1,0:T(8,128)(2,1)S(1)}, bf16[256,8192]{1,0:T(8,128)(2,1)}, u32[]{:S(2)}) copy-start(bf16[256,8192]{1,0:T(8,128)(2,1)} %param.11) | copy-start | bytes 12582916
  19.1 0.7 copy-start.3
  19.1 43.2 %copy-start.2 = (bf16[8,64,256]{2,1,0:T(8,128)(2,1)S(1)}, bf16[8,64,256]{2,1,0:T(8,128)(2,1)}, u32[]{:S(2)}) copy-start(bf16[8,64,256]{2,1,0:T(8,128)(2,1)} %param.13) | copy-start | bytes 786436
Sparse Core Ops, SparseCore 0:
  19.2 143.6 reduce-scatter.1
where the time goes:
time: 172 us; the launch traced here: 171 us
  waiting for transfers between devices  100 us (58%)
  blocking collectives  42.3 us (25%)
  between operations  13.4 us (8%)
  matrix products  11.4 us (7%)
  local copies, waits for them, and re-layouts  2.28 us (1%)
    reduce_scatter x1, waiting for transfers between devices, body(): lax.psum_scatter(lax.dot_general(output_projection_weight, attended_state...  100 us
    psum x1, blocking collectives, body(): low_rank_state = lax.psum(partial_low, 'tensor').astype(jnp.bfloat16)  42.3 us
    sub x1, matrix products, body(): expd = jnp.exp(scores - top)  4.63 us
    dot_general x1, matrix products, body(): jnp.einsum('rht,rte->rhe', weights, values_local, preferred_element_type=...  3.59 us
  transfers between devices with their start and end apart: 1, of which 1 were waited for; matrix products, arithmetic and copies ran while one was open for 0% of the time, Pallas kernels for 0%

commit v1 on v0

v1 whole, which is shorter than its diff:
```python
import math

import jax
import jax.numpy as jnp
from jax import lax
from jax.experimental import pallas as pl
from jax.experimental.pallas import tpu as pltpu
from jax.sharding import PartitionSpec as P

HEAD = 128
PIECES = 2
CHUNK = 16
MESH = pl.DeviceIdType.MESH
F32 = jnp.float32
BF16 = jnp.bfloat16
NEG = -1e30


def kernel(
    q_ref, len_ref, idx_ref, cache_hbm, w_hbm, down_hbm, up_hbm, out_ref,
    cache, w, down, up, lens, picks, att,
    sent1, own, got1, sent2, kept1, got2, sent3, kept2, got3, sent4, got4,
    low0, low1, low2, low3, lg1, lg2, lg3, lg4,
    load_sem, send_sem, recv_sem,
):
    rows = q_ref.shape[0]
    half = rows // PIECES
    chunks = rows // CHUNK
    slots = cache.shape[1]
    count = down.shape[0]
    rank = down.shape[2]
    out_width = up.shape[2]

    me = lax.axis_index("tensor")
    core = me % 2
    xx = (me // 2) % 2
    yy = (me // 4) % 2
    zz = me // 8
    core_peer = me + 1 - 2 * core
    x_peer = me + 2 - 4 * xx
    y_peer = me + 4 - 8 * yy
    z_others = (zz + 1 - 2 * (zz % 2), (zz + 2) % 4, 3 - zz)
    z_peers = tuple(me + 8 * (other - zz) for other in z_others)
    peers = (core_peer, x_peer, y_peer) + z_peers

    cache_loads = [
        pltpu.make_async_copy(
            cache_hbm.at[0, pl.ds(c * CHUNK, CHUNK)],
            cache.at[pl.ds(c * CHUNK, CHUNK)],
            load_sem.at[c],
        )
        for c in range(chunks)
    ]
    down_load = pltpu.make_async_copy(down_hbm, down, load_sem.at[chunks])
    up_load = pltpu.make_async_copy(up_hbm, up, load_sem.at[chunks + 1])
    w_load = pltpu.make_async_copy(w_hbm, w, load_sem.at[chunks + 2])
    for c in range(chunks // 2):
        cache_loads[c].start()
    down_load.start()
    w_load.start()
    for c in range(chunks // 2, chunks):
        cache_loads[c].start()
    up_load.start()

    barrier = pltpu.get_barrier_semaphore()
    for peer in peers:
        pl.semaphore_signal(barrier, inc=1, device_id={"tensor": peer}, device_id_type=MESH)

    def send(p, step, src, dst, peer):
        return pltpu.make_async_remote_copy(
            src_ref=src,
            dst_ref=dst,
            send_sem=send_sem.at[p, step],
            recv_sem=recv_sem.at[p, step],
            device_id={"tensor": peer},
            device_id_type=MESH,
        )

    lens[...] = jnp.transpose(jnp.broadcast_to(len_ref[...].astype(F32), (slots, rows)))
    picks[...] = jnp.transpose(jnp.broadcast_to(idx_ref[...].astype(F32), (out_width, rows)))

    row_of = lax.broadcasted_iota(jnp.int32, (2 * CHUNK, slots), 0) % CHUNK
    slot_of = lax.broadcasted_iota(jnp.int32, (2 * CHUNK, slots), 1).astype(F32)
    scale = 1.0 / math.sqrt(HEAD)

    def attend(c, carry):
        at = pl.multiple_of(c * CHUNK, CHUNK)
        pltpu.make_async_copy(
            cache_hbm.at[0, pl.ds(at, CHUNK)], cache.at[pl.ds(at, CHUNK)], load_sem.at[c]
        ).wait()
        block = cache[pl.ds(at, CHUNK)].reshape(CHUNK * slots, 2 * HEAD)
        q = q_ref[pl.ds(at, CHUNK), :]
        q = jnp.concatenate([q[:, :HEAD], q[:, HEAD:]], axis=0)
        raw = lax.dot_general(
            q, block[:, :HEAD], (((1,), (1,)), ((), ())), preferred_element_type=F32
        )
        scores = raw[:, :slots]
        for r in range(1, CHUNK):
            scores = jnp.where(row_of == r, raw[:, r * slots : (r + 1) * slots], scores)
        live = lens[pl.ds(at, CHUNK), :]
        live = jnp.concatenate([live, live], axis=0)
        scores = jnp.where(slot_of < live, scores * scale, NEG)
        top = jnp.max(scores, axis=-1, keepdims=True)
        expd = jnp.exp(scores - top)
        weights = expd / jnp.sum(expd, axis=-1, keepdims=True)
        spread = jnp.concatenate(
            [jnp.where(row_of == r, weights, 0.0).astype(BF16) for r in range(CHUNK)], axis=1
        )
        mixed = jnp.dot(spread, block[:, HEAD:], preferred_element_type=F32).astype(BF16)
        att[pl.ds(at, CHUNK), :HEAD] = mixed[:CHUNK]
        att[pl.ds(at, CHUNK), HEAD:] = mixed[CHUNK:]
        return carry

    def fold(low):
        return jnp.concatenate([low[: half // 2], low[half // 2 :]], axis=1)

    def unfold(low):
        return jnp.concatenate([low[:, :rank], low[:, rank:]], axis=0)

    first_peer = (x_peer, y_peer)
    second_peer = (y_peer, x_peer)
    first = (xx, yy)
    second = (yy, xx)
    first_step = (2, 4)
    second_step = (4, 2)

    def columns(p, i, side):
        index = (i % 4) * 8 + (i // 8) * first_step[p] + ((i // 4) % 2) * second_step[p] + side
        return pl.ds(pl.multiple_of(index * out_width, out_width), out_width)

    def low_part(p):
        piece = att[p * half : (p + 1) * half, :].astype(F32)
        pick = picks[p * half : (p + 1) * half, :]
        total = jnp.zeros((half, rank), F32)
        for a in range(count):
            chosen = jnp.where(pick == a, piece, 0.0).astype(BF16)
            total = total + jnp.dot(chosen, down[a], preferred_element_type=F32)
        low0[p] = fold(total)
        copy = send(p, 6, low0.at[p], lg1.at[p], core_peer)
        copy.start()
        return copy

    def project(p):
        def far(i, carry):
            sent1[p, i] = jnp.dot(
                att[p * half : (p + 1) * half, :], w[:, columns(p, i, 1 - core)],
                preferred_element_type=F32,
            ).astype(BF16)
            return carry

        def near(i, carry):
            own[p, i] = jnp.dot(
                att[p * half : (p + 1) * half, :], w[:, columns(p, i, core)],
                preferred_element_type=F32,
            )
            return carry

        lax.fori_loop(0, 16, far, 0)
        copy = send(p, 0, sent1.at[p], got1.at[p], core_peer)
        copy.start()
        lax.fori_loop(0, 16, near, 0)
        return copy

    def along_first(p, copy, low_copy):
        low_copy.wait()
        low1[p] = low0[p] + lg1[p]
        low_next = send(p, 7, low1.at[p], lg2.at[p], first_peer[p])
        low_next.start()
        copy.wait()
        mine, other = first[p] * 8, (1 - first[p]) * 8

        def give(j, carry):
            sent2[p, j] = (own[p, other + j] + got1[p, other + j].astype(F32)).astype(BF16)
            return carry

        def keep(j, carry):
            kept1[p, j] = own[p, mine + j] + got1[p, mine + j].astype(F32)
            return carry

        lax.fori_loop(0, 8, give, 0)
        following = send(p, 1, sent2.at[p], got2.at[p], first_peer[p])
        following.start()
        lax.fori_loop(0, 8, keep, 0)
        return following, low_next

    def along_second(p, copy, low_copy):
        low_copy.wait()
        low2[p] = low1[p] + lg2[p]
        low_next = send(p, 8, low2.at[p], lg3.at[p], second_peer[p])
        low_next.start()
        copy.wait()
        mine, other = second[p] * 4, (1 - second[p]) * 4

        def give(j, carry):
            sent3[p, j] = (kept1[p, other + j] + got2[p, other + j].astype(F32)).astype(BF16)
            return carry

        def keep(j, carry):
            kept2[p, j] = kept1[p, mine + j] + got2[p, mine + j].astype(F32)
            return carry

        lax.fori_loop(0, 4, give, 0)
        following = send(p, 2, sent3.at[p], got3.at[p], second_peer[p])
        following.start()
        lax.fori_loop(0, 4, keep, 0)
        return following, low_next

    def along_z(p, copy, low_copy):
        low_copy.wait()
        low3[p] = low2[p] + lg3[p]
        copies = []
        for k in range(3):
            copies.append(send(p, 9 + k, low3.at[p], lg4.at[p, k], z_peers[k]))
            copies[-1].start()
        copy.wait()
        for k in (1, 2, 0):
            to = z_others[k]
            sent4[p, k] = (kept2[p, to] + got3[p, to].astype(F32)).astype(BF16)
            copies.append(send(p, 3 + k, sent4.at[p, k], got4.at[p, k], z_peers[k]))
            copies[-1].start()
        return copies

    def finish(p, copies):
        for copy in copies[:3]:
            copy.wait()
        low = unfold(low3[p] + lg4[p, 0] + (lg4[p, 1] + lg4[p, 2]))
        low = low.astype(BF16).astype(F32)
        pick = picks[p * half : (p + 1) * half, :rank]
        total = kept2[p, zz] + got3[p, zz].astype(F32)
        for a in range(count):
            chosen = jnp.where(pick == a, low, 0.0).astype(BF16)
            total = total + jnp.dot(chosen, up[a], preferred_element_type=F32)
        for copy in copies[3:]:
            copy.wait()
        for k in range(3):
            total = total + got4[p, k].astype(F32)
        return total

    lax.fori_loop(0, chunks // 2, attend, 0)
    down_load.wait()
    pl.semaphore_wait(barrier, len(peers))
    low_a = low_part(0)
    w_load.wait()
    a = project(0)
    lax.fori_loop(chunks // 2, chunks, attend, 0)
    low_b = low_part(1)
    a, low_a = along_first(0, a, low_a)
    b = project(1)
    b, low_b = along_first(1, b, low_b)
    a, low_a = along_second(0, a, low_a)
    b, low_b = along_second(1, b, low_b)
    a = along_z(0, a, low_a)
    b = along_z(1, b, low_b)
    up_load.wait()
    top = finish(0, a)
    bottom = finish(1, b)
    out_ref[...] = jnp.transpose(jnp.concatenate([top, bottom], axis=0)).astype(BF16)


def body(
    queries,
    cache,
    lengths,
    request_adapter_index,
    output_projection_weight,
    adapter_down_weight,
    adapter_up_weight,
):
    downs, ups = (
        lax.all_gather(adapter_down_weight, "dp", axis=0, tiled=True),
        lax.all_gather(adapter_up_weight, "dp", axis=0, tiled=True),
    )
    rows = queries.shape[0]
    half = rows // PIECES
    chunks = rows // CHUNK
    slots = cache.shape[2]
    width = ups.shape[2]
    rank = downs.shape[2]
    low = (PIECES, half // 2, 2 * rank)

    def blocks(n, kind=BF16):
        return pltpu.VMEM((PIECES, n, half, width), kind)

    vmem = pl.BlockSpec(memory_space=pltpu.VMEM)
    hbm = pl.BlockSpec(memory_space=pl.ANY)
    return pl.pallas_call(
        kernel,
        out_shape=jax.ShapeDtypeStruct((width, rows), BF16),
        in_specs=[vmem, vmem, vmem, hbm, hbm, hbm, hbm],
        out_specs=vmem,
        scratch_shapes=[
            pltpu.VMEM(cache.shape[1:], BF16),
            pltpu.VMEM(output_projection_weight.shape, BF16),
            pltpu.VMEM(downs.shape, BF16),
            pltpu.VMEM(ups.shape, BF16),
            pltpu.VMEM((rows, slots), F32),
            pltpu.VMEM((rows, width), F32),
            pltpu.VMEM((rows, queries.shape[1]), BF16),
            blocks(16), blocks(16, F32), blocks(16),
            blocks(8), blocks(8, F32), blocks(8),
            blocks(4), blocks(4, F32), blocks(4),
            blocks(3), blocks(3),
            pltpu.VMEM(low, F32), pltpu.VMEM(low, F32), pltpu.VMEM(low, F32), pltpu.VMEM(low, F32),
            pltpu.VMEM(low, F32), pltpu.VMEM(low, F32), pltpu.VMEM(low, F32),
            pltpu.VMEM((PIECES, 3) + low[1:], F32),
            pltpu.SemaphoreType.DMA((chunks + 3,)),
            pltpu.SemaphoreType.DMA((PIECES, 12)),
            pltpu.SemaphoreType.DMA((PIECES, 12)),
        ],
        compiler_params=pltpu.CompilerParams(
            collective_id=0, has_side_effects=True, vmem_limit_bytes=48 * 1024 * 1024
        ),
    )(
        queries,
        lengths.reshape(1, rows),
        request_adapter_index.reshape(1, rows),
        cache,
        output_projection_weight,
        downs,
        ups,
    )


def solution(mesh):
    return jax.shard_map(
        body,
        mesh=mesh,
        in_specs=(
            P(("groups", "dp"), "tensor"),
            P("tensor", ("groups", "dp"), None, None),
            P(("groups", "dp")),
            P(("groups", "dp")),
            P("tensor", None),
            P(("groups", "dp"), "tensor", None),
            P(("groups", "dp"), None, "tensor"),
        ),
        out_specs=P("tensor", ("groups", "dp")),
        check_vma=False,
    )
```

time: 172 us -> 47.5 us (0.28)
  waiting for transfers between devices: 100 us -> 0 us
  blocking collectives: 42.3 us -> 0 us
  Pallas kernels: 0 us -> 40 us
  between operations: 13.4 us -> 0.03 us
  matrix products: 11.4 us -> 0 us
  local copies, waits for them, and re-layouts: 2.28 us -> 7.14 us
    reduce_scatter x1 -> x0, waiting for transfers between devices: 100 us -> none  [body(): lax.psum_scatter(lax.dot_general(output_projection_weight, attended_state...]
    psum x1 -> x0, blocking collectives: 42.3 us -> none  [body(): low_rank_state = lax.psum(partial_low, 'tensor').astype(jnp.bfloat16)]
    pallas_call x0 -> x1, Pallas kernels: none -> 40 us  [body(): pl.pallas_call(kernel, out_shape=jax.ShapeDtypeStruct((width, rows), BF16...]
    dot_general x3 -> x0, matrix products: 6.57 us -> none  [the longest x1 3.59 us: body(): jnp.einsum('rht,rte->rhe', weights, values_local, preferred_element_type=...]
    unnamed x8 -> x12, local copies, waits for them, and re-layouts: 0.64 us -> 7.14 us
    sub x1 -> x0, matrix products: 4.63 us -> none  [body(): expd = jnp.exp(scores - top)]
  transfers between devices with their start and end apart: 1 -> 0, of which waited for: 1 -> 0; matrix products, arithmetic and copies ran while one was open for 0% -> 0% of each run, Pallas kernels for 0% -> 0%
where the time goes in v1:
time: 47.5 us; the launch traced here: 47.2 us
  Pallas kernels  40 us (84%)
  local copies, waits for them, and re-layouts  7.14 us (15%)
    pallas_call x1, Pallas kernels, body(): pl.pallas_call(kernel, out_shape=jax.ShapeDtypeStruct((width, rows), BF16...  40 us
    unnamed x12, local copies, waits for them, and re-layouts  7.14 us

profile of v1, /device:TPU:0, one launch (start us, length us, event | category | flops | bytes accessed | tf_op | source)
XLA Modules:
  0.0 47.2 jit_solution(11238163381911599617)
XLA Ops:
  0.0 1.2 %copy.8.down_hbm = bf16[8,256,64]{2,1,0:T(8,128)(2,1)S(1)} copy(bf16[8,256,64]{1,2,0:T(8,128)(2,1)} %param.12) | data formatting | bytes 524288 | tf_op args[5]
  1.2 0.0 copy-start
  1.2 2.2 %copy-done = bf16[256,8192]{1,0:T(8,128)(2,1)S(1)} copy-done((bf16[256,8192]{1,0:T(8,128)(2,1)S(1)}, bf16[256,8192]{1,0:T(8,128)(2,1)}, u32[]{:S(2)}) %copy-start) | copy-done | bytes 4194328
  3.4 0.0 copy-start.1
  3.4 0.9 %copy-done.1 = bf16[8,64,256]{2,1,0:T(8,128)(2,1)S(1)} copy-done((bf16[8,64,256]{2,1,0:T(8,128)(2,1)S(1)}, bf16[8,64,256]{2,1,0:T(8,128)(2,1)}, u32[]{:S(2)}) %copy-start.1) | copy-done | bytes 262168
  4.4 0.0 copy-start.2
  4.4 0.8 %copy-done.2 = bf16[128,256]{1,0:T(8,128)(2,1)S(1)} copy-done((bf16[128,256]{1,0:T(8,128)(2,1)S(1)}, bf16[128,256]{1,0:T(8,128)(2,1)}, u32[]{:S(2)}) %copy-start.2) | copy-done | bytes 65560
  5.2 0.0 copy-start.3
  5.2 0.7 %copy-done.3 = s32[128]{0:T(128)S(1)} copy-done((s32[128]{0:T(128)S(1)}, s32[128]{0:T(128)}, u32[]{:S(2)}) %copy-start.3) | copy-done | bytes 536
  5.9 0.0 copy-start.4
  5.9 0.7 %copy-done.4 = s32[128]{0:T(128)S(1)} copy-done((s32[128]{0:T(128)S(1)}, s32[128]{0:T(128)}, u32[]{:S(2)}) %copy-start.4) | copy-done | bytes 536
  6.5 40.0 %shard_map.73 = bf16[256,128]{1,0:T(8,128)(2,1)S(1)} custom-call(bf16[128,256]{1,0:T(8,128)(2,1)S(1)} %copy-done.2, s32[1,128]{1,0:T(1,128)S(1)} %bitcast.2, s32[1,128]{1,0:T(1,128)S(1)} %bitcast.3, bf16[1,128,128,256]{3,2,1,0:T(8,128)(2,1)} %cache_hbm.1, bf16[256,8192]{1,0:T(8,128)(2,1)S(1)} %copy-done, bf16[8,256,64]{2,1,0:T(8,128)(2,1)S(1)} %copy.8.down_hbm, ...), custom_call_target="tpu_custom_call" | custom-call | tf_op jit(solution)/shard_map/pallas_call | solution.py:286
  46.6 0.6 %copy.10 = bf16[256,128]{1,0:T(8,128)(2,1)} copy(bf16[256,128]{1,0:T(8,128)(2,1)S(1)} %shard_map.73) | data formatting | bytes 131072
Async XLA Ops:
  1.2 2.2 %copy-start = (bf16[256,8192]{1,0:T(8,128)(2,1)S(1)}, bf16[256,8192]{1,0:T(8,128)(2,1)}, u32[]{:S(2)}) copy-start(bf16[256,8192]{1,0:T(8,128)(2,1)} %w_hbm.1) | copy-start | bytes 12582916
  3.4 0.9 %copy-start.1 = (bf16[8,64,256]{2,1,0:T(8,128)(2,1)S(1)}, bf16[8,64,256]{2,1,0:T(8,128)(2,1)}, u32[]{:S(2)}) copy-start(bf16[8,64,256]{2,1,0:T(8,128)(2,1)} %up_hbm) | copy-start | bytes 786436
  4.4 0.8 %copy-start.2 = (bf16[128,256]{1,0:T(8,128)(2,1)S(1)}, bf16[128,256]{1,0:T(8,128)(2,1)}, u32[]{:S(2)}) copy-start(bf16[128,256]{1,0:T(8,128)(2,1)} %q_ref.1) | copy-start | bytes 196612
  5.2 0.7 %copy-start.3 = (s32[128]{0:T(128)S(1)}, s32[128]{0:T(128)}, u32[]{:S(2)}) copy-start(s32[128]{0:T(128)} %param.9) | copy-start | bytes 1540
  5.9 0.7 %copy-start.4 = (s32[128]{0:T(128)S(1)}, s32[128]{0:T(128)}, u32[]{:S(2)}) copy-start(s32[128]{0:T(128)} %param.10) | copy-start | bytes 1540

commit v2 on v1

v2 whole, which is shorter than its diff:
```python
import math

import jax
import jax.numpy as jnp
from jax import lax
from jax.experimental import pallas as pl
from jax.experimental.pallas import tpu as pltpu
from jax.sharding import PartitionSpec as P

HEAD = 128
PIECES = 2
CHUNK = 16
MESH = pl.DeviceIdType.MESH
F32 = jnp.float32
BF16 = jnp.bfloat16
NEG = -1e30


def kernel(
    q_hbm, len_hbm, idx_hbm, cache_hbm, w_hbm, down_hbm, up_hbm, out_ref,
    q_ref, len_ref, idx_ref, cache, w, down, up, lens, picks, att,
    sent1, own, got1, sent2, kept1, got2, sent3, kept2, got3, sent4, got4,
    low0, low1, low2, low3, lg1, lg2, lg3, lg4,
    load_sem, send_sem, recv_sem,
):
    rows = q_hbm.shape[0]
    half = rows // PIECES
    chunks = rows // CHUNK
    slots = cache.shape[1]
    count = down.shape[0]
    rank = down.shape[1]
    out_width = up.shape[2]

    me = lax.axis_index("tensor")
    core = me % 2
    xx = (me // 2) % 2
    yy = (me // 4) % 2
    zz = me // 8
    core_peer = me + 1 - 2 * core
    x_peer = me + 2 - 4 * xx
    y_peer = me + 4 - 8 * yy
    z_others = (zz + 1 - 2 * (zz % 2), (zz + 2) % 4, 3 - zz)
    z_peers = tuple(me + 8 * (other - zz) for other in z_others)
    peers = (core_peer, x_peer, y_peer) + z_peers

    cache_loads = [
        pltpu.make_async_copy(
            cache_hbm.at[0, pl.ds(c * CHUNK, CHUNK)],
            cache.at[pl.ds(c * CHUNK, CHUNK)],
            load_sem.at[c],
        )
        for c in range(chunks)
    ]
    down_load = pltpu.make_async_copy(down_hbm, down, load_sem.at[chunks])
    up_load = pltpu.make_async_copy(up_hbm, up, load_sem.at[chunks + 1])
    w_load = pltpu.make_async_copy(w_hbm, w, load_sem.at[chunks + 2])
    small_loads = [
        pltpu.make_async_copy(src, dst, load_sem.at[chunks + 3 + i])
        for i, (src, dst) in enumerate(((q_hbm, q_ref), (len_hbm, len_ref), (idx_hbm, idx_ref)))
    ]
    for load in small_loads:
        load.start()
    for c in range(chunks // 2):
        cache_loads[c].start()
    down_load.start()
    w_load.start()
    for c in range(chunks // 2, chunks):
        cache_loads[c].start()
    up_load.start()

    barrier = pltpu.get_barrier_semaphore()
    for peer in peers:
        pl.semaphore_signal(barrier, inc=1, device_id={"tensor": peer}, device_id_type=MESH)

    def send(p, step, src, dst, peer):
        return pltpu.make_async_remote_copy(
            src_ref=src,
            dst_ref=dst,
            send_sem=send_sem.at[p, step],
            recv_sem=recv_sem.at[p, step],
            device_id={"tensor": peer},
            device_id_type=MESH,
        )

    for load in small_loads:
        load.wait()
    lens[...] = jnp.transpose(jnp.broadcast_to(len_ref[...].astype(F32), (slots, rows)))
    picks[...] = jnp.transpose(jnp.broadcast_to(idx_ref[...].astype(F32), (out_width, rows)))

    row_of = lax.broadcasted_iota(jnp.int32, (2 * CHUNK, slots), 0) % CHUNK
    slot_of = lax.broadcasted_iota(jnp.int32, (2 * CHUNK, slots), 1).astype(F32)
    scale = 1.0 / math.sqrt(HEAD)

    def attend(c, carry):
        at = pl.multiple_of(c * CHUNK, CHUNK)
        pltpu.make_async_copy(
            cache_hbm.at[0, pl.ds(at, CHUNK)], cache.at[pl.ds(at, CHUNK)], load_sem.at[c]
        ).wait()
        block = cache[pl.ds(at, CHUNK)].reshape(CHUNK * slots, 2 * HEAD)
        q = q_ref[pl.ds(at, CHUNK), :]
        q = jnp.concatenate([q[:, :HEAD], q[:, HEAD:]], axis=0)
        raw = lax.dot_general(
            q, block[:, :HEAD], (((1,), (1,)), ((), ())), preferred_element_type=F32
        )
        scores = raw[:, :slots]
        for r in range(1, CHUNK):
            scores = jnp.where(row_of == r, raw[:, r * slots : (r + 1) * slots], scores)
        live = lens[pl.ds(at, CHUNK), :]
        live = jnp.concatenate([live, live], axis=0)
        scores = jnp.where(slot_of < live, scores * scale, NEG)
        top = jnp.max(scores, axis=-1, keepdims=True)
        expd = jnp.exp(scores - top)
        weights = expd / jnp.sum(expd, axis=-1, keepdims=True)
        spread = jnp.concatenate(
            [jnp.where(row_of == r, weights, 0.0).astype(BF16) for r in range(CHUNK)], axis=1
        )
        mixed = jnp.dot(spread, block[:, HEAD:], preferred_element_type=F32).astype(BF16)
        att[pl.ds(at, CHUNK), :HEAD] = mixed[:CHUNK]
        att[pl.ds(at, CHUNK), HEAD:] = mixed[CHUNK:]
        return carry

    def fold(low):
        return jnp.concatenate([low[: half // 2], low[half // 2 :]], axis=1)

    def unfold(low):
        return jnp.concatenate([low[:, :rank], low[:, rank:]], axis=0)

    first_peer = (x_peer, y_peer)
    second_peer = (y_peer, x_peer)
    z_order = (z_others[1], z_others[2], z_others[0], zz)
    z_slot_peers = (z_peers[1], z_peers[2], z_peers[0])

    def group_of(p, dx, dy):
        return dx * 2 + dy if p == 0 else dy * 2 + dx

    def low_part(p):
        piece = att[p * half : (p + 1) * half, :].astype(F32)
        pick = picks[p * half : (p + 1) * half, :]
        total = jnp.zeros((half, rank), F32)
        for a in range(count):
            chosen = jnp.where(pick == a, piece, 0.0).astype(BF16)
            total = total + lax.dot_general(
                chosen, down[a], (((1,), (1,)), ((), ())), preferred_element_type=F32
            )
        low0[p] = fold(total)
        copy = send(p, 6, low0.at[p], lg1.at[p], core_peer)
        copy.start()
        return copy

    def product(dx, dy, side, slot):
        x_at = xx + dx * (1 - 2 * xx)
        y_at = yy + dy * (1 - 2 * yy)
        index = z_order[slot] * 8 + y_at * 4 + x_at * 2 + side
        columns = pl.ds(pl.multiple_of(index * out_width, out_width), out_width)
        return jnp.dot(att[...], w[:, columns], preferred_element_type=F32)

    def far(dx, dy):
        places = (group_of(0, dx, dy), group_of(1, dx, dy))
        for slot in range(4):
            block = product(dx, dy, 1 - core, slot).astype(BF16)
            for p in range(PIECES):
                sent1[p, places[p] * 4 + slot] = block[p * half : (p + 1) * half]
        copies = []
        for p in range(PIECES):
            at = pl.ds(places[p] * 4, 4)
            copies.append(send(p, 12 + places[p], sent1.at[p, at], got1.at[p, at], core_peer))
            copies[-1].start()
        return copies

    def near(dx, dy, copies):
        places = (group_of(0, dx, dy), group_of(1, dx, dy))
        for slot in range(4):
            block = product(dx, dy, core, slot)
            for p in range(PIECES):
                own[p, places[p] * 4 + slot] = block[p * half : (p + 1) * half]
        following = [None] * PIECES
        for p in range(PIECES):
            place = places[p]
            copies[p].wait()
            to = (place % 2) * 4
            for slot in range(4):
                total = own[p, place * 4 + slot] + got1[p, place * 4 + slot].astype(F32)
                if place >= 2:
                    sent2[p, to + slot] = total.astype(BF16)
                else:
                    kept1[p, to + slot] = total
            if place >= 2:
                at = pl.ds(to, 4)
                following[p] = send(p, place % 2, sent2.at[p, at], got2.at[p, at], first_peer[p])
                following[p].start()
        return following

    def low_second(p, copy):
        copy.wait()
        low1[p] = low0[p] + lg1[p]
        following = send(p, 7, low1.at[p], lg2.at[p], first_peer[p])
        following.start()
        return following

    def low_third(p, copy):
        copy.wait()
        low2[p] = low1[p] + lg2[p]
        following = send(p, 8, low2.at[p], lg3.at[p], second_peer[p])
        following.start()
        return following

    def low_last(p, copy):
        copy.wait()
        low3[p] = low2[p] + lg3[p]
        copies = []
        for k in range(3):
            copies.append(send(p, 9 + k, low3.at[p], lg4.at[p, k], z_peers[k]))
            copies[-1].start()
        return copies

    def along_second(p, copy):
        copy.wait()
        following = []
        for part in range(2):
            for slot in (2 * part, 2 * part + 1):
                sent3[p, slot] = (kept1[p, 4 + slot] + got2[p, 4 + slot].astype(F32)).astype(BF16)
            at = pl.ds(2 * part, 2)
            following.append(
                send(p, 2 + 14 * part, sent3.at[p, at], got3.at[p, at], second_peer[p])
            )
            following[-1].start()
        return following

    def keep_second(p, copy):
        copy.wait()
        for slot in range(4):
            kept2[p, slot] = kept1[p, slot] + got2[p, slot].astype(F32)

    def along_z(p, part, copy):
        copy.wait()
        copies = []
        for slot in (0, 1) if part == 0 else (2,):
            sent4[p, slot] = (kept2[p, slot] + got3[p, slot].astype(F32)).astype(BF16)
            copies.append(
                send(p, 3 + slot, sent4.at[p, slot], got4.at[p, slot], z_slot_peers[slot])
            )
            copies[-1].start()
        return copies

    def finish(p, low_copies):
        for copy in low_copies:
            copy.wait()
        low = unfold(low3[p] + lg4[p, 0] + (lg4[p, 1] + lg4[p, 2]))
        low = low.astype(BF16).astype(F32)
        pick = picks[p * half : (p + 1) * half, :rank]
        total = kept2[p, 3] + got3[p, 3].astype(F32)
        for a in range(count):
            chosen = jnp.where(pick == a, low, 0.0).astype(BF16)
            total = total + jnp.dot(chosen, up[a], preferred_element_type=F32)
        return total

    pieces = range(PIECES)
    lax.fori_loop(0, chunks, attend, 0)
    pl.semaphore_wait(barrier, len(peers))
    w_load.wait()
    crossing = {}
    crossing[1, 1] = far(1, 1)
    down_load.wait()
    low = [low_part(p) for p in pieces]
    for key in ((1, 0), (0, 1), (0, 0)):
        crossing[key] = far(*key)
    early = near(1, 1, crossing[1, 1])
    low = [low_second(p, low[p]) for p in pieces]
    late = [None] * PIECES
    late[0] = near(1, 0, crossing[1, 0])[0]
    late[1] = near(0, 1, crossing[0, 1])[1]
    low = [low_third(p, low[p]) for p in pieces]
    near(0, 0, crossing[0, 0])
    turned = [along_second(p, early[p]) for p in pieces]
    low = [low_last(p, low[p]) for p in pieces]
    for p in pieces:
        keep_second(p, late[p])
    last = [along_z(p, 0, turned[p][0]) for p in pieces]
    for p in pieces:
        last[p] = last[p] + along_z(p, 1, turned[p][1])
    up_load.wait()
    totals = [finish(p, low[p]) for p in pieces]
    for p in pieces:
        for copy in last[p]:
            copy.wait()
        for slot in range(3):
            totals[p] = totals[p] + got4[p, slot].astype(F32)
    out_ref[...] = jnp.transpose(jnp.concatenate(totals, axis=0)).astype(BF16)


def body(
    queries,
    cache,
    lengths,
    request_adapter_index,
    output_projection_weight,
    adapter_down_weight,
    adapter_up_weight,
):
    downs, ups = (
        lax.all_gather(adapter_down_weight, "dp", axis=0, tiled=True),
        lax.all_gather(adapter_up_weight, "dp", axis=0, tiled=True),
    )
    rows = queries.shape[0]
    half = rows // PIECES
    chunks = rows // CHUNK
    slots = cache.shape[2]
    width = ups.shape[2]
    downs = jnp.transpose(downs, (0, 2, 1))
    rank = downs.shape[1]
    low = (PIECES, half // 2, 2 * rank)

    def blocks(n, kind=BF16):
        return pltpu.VMEM((PIECES, n, half, width), kind)

    vmem = pl.BlockSpec(memory_space=pltpu.VMEM)
    hbm = pl.BlockSpec(memory_space=pltpu.HBM)
    return pl.pallas_call(
        kernel,
        out_shape=jax.ShapeDtypeStruct((width, rows), BF16),
        in_specs=[hbm] * 7,
        out_specs=vmem,
        scratch_shapes=[
            pltpu.VMEM(queries.shape, BF16),
            pltpu.VMEM((1, rows), jnp.int32),
            pltpu.VMEM((1, rows), jnp.int32),
            pltpu.VMEM(cache.shape[1:], BF16),
            pltpu.VMEM(output_projection_weight.shape, BF16),
            pltpu.VMEM(downs.shape, BF16),
            pltpu.VMEM(ups.shape, BF16),
            pltpu.VMEM((rows, slots), F32),
            pltpu.VMEM((rows, width), F32),
            pltpu.VMEM((rows, queries.shape[1]), BF16),
            blocks(16), blocks(16, F32), blocks(16),
            blocks(8), blocks(8, F32), blocks(8),
            blocks(4), blocks(4, F32), blocks(4),
            blocks(3), blocks(3),
            pltpu.VMEM(low, F32), pltpu.VMEM(low, F32), pltpu.VMEM(low, F32), pltpu.VMEM(low, F32),
            pltpu.VMEM(low, F32), pltpu.VMEM(low, F32), pltpu.VMEM(low, F32),
            pltpu.VMEM((PIECES, 3) + low[1:], F32),
            pltpu.SemaphoreType.DMA((chunks + 6,)),
            pltpu.SemaphoreType.DMA((PIECES, 17)),
            pltpu.SemaphoreType.DMA((PIECES, 17)),
        ],
        compiler_params=pltpu.CompilerParams(
            collective_id=0, has_side_effects=True, vmem_limit_bytes=56 * 1024 * 1024
        ),
    )(
        queries,
        lengths.reshape(1, rows),
        request_adapter_index.reshape(1, rows),
        cache,
        output_projection_weight,
        downs,
        ups,
    )


def solution(mesh):
    return jax.shard_map(
        body,
        mesh=mesh,
        in_specs=(
            P(("groups", "dp"), "tensor"),
            P("tensor", ("groups", "dp"), None, None),
            P(("groups", "dp")),
            P(("groups", "dp")),
            P("tensor", None),
            P(("groups", "dp"), "tensor", None),
            P(("groups", "dp"), None, "tensor"),
        ),
        out_specs=P("tensor", ("groups", "dp")),
        check_vma=False,
    )
```

time: 47.5 us -> 32.6 us (0.69)
  Pallas kernels: 40 us -> 31 us
  local copies, waits for them, and re-layouts: 7.14 us -> 1.47 us
    pallas_call x1, Pallas kernels: 40 us -> 31 us  [body(): pl.pallas_call(kernel, out_shape=jax.ShapeDtypeStruct((width, rows), BF16...]
    unnamed x12 -> x1, local copies, waits for them, and re-layouts: 7.14 us -> 1.47 us
where the time goes in v2:
time: 32.6 us; the launch traced here: 32.4 us
  Pallas kernels  31 us (95%)
  local copies, waits for them, and re-layouts  1.47 us (5%)
    pallas_call x1, Pallas kernels, body(): pl.pallas_call(kernel, out_shape=jax.ShapeDtypeStruct((width, rows), BF16...  31 us
    unnamed x1, local copies, waits for them, and re-layouts  1.47 us

profile of v2, /device:TPU:0, one launch (start us, length us, event | category | flops | bytes accessed | tf_op | source)
XLA Modules:
  0.0 32.4 jit_solution(6827639673195009148)
XLA Ops:
  0.0 31.0 %shard_map.73 = bf16[256,128]{1,0:T(8,128)(2,1)} custom-call(bf16[128,256]{1,0:T(8,128)(2,1)} %q_hbm.1, s32[1,128]{1,0:T(1,128)} %bitcast.4, s32[1,128]{1,0:T(1,128)} %bitcast.5, bf16[1,128,128,256]{3,2,1,0:T(8,128)(2,1)} %cache_hbm.1, bf16[256,8192]{1,0:T(8,128)(2,1)} %w_hbm.1, bf16[8,64,256]{2,1,0:T(8,128)(2,1)} %bitcast.3, bf16[8,64,256]{2,1,0:T(8,128)(2,1)} %up_hbm), custom_call_target="tpu_custom_call" | custom-call | tf_op jit(solution)/shard_map/pallas_call | solution.py:318
  31.0 1.5 %copy.9 = bf16[256,128]{1,0:T(8,128)(2,1)} copy(bf16[256,128]{1,0:T(8,128)(2,1)} %shard_map.73) | data formatting | bytes 131072

commit v3 on v2

--- a/solution.py
+++ b/solution.py
@@ -257,22 +257,23 @@
     pieces = range(PIECES)
     lax.fori_loop(0, chunks, attend, 0)
     pl.semaphore_wait(barrier, len(peers))
+    down_load.wait()
+    low = [low_part(p) for p in pieces]
     w_load.wait()
     crossing = {}
+    late = [None] * PIECES
     crossing[1, 1] = far(1, 1)
-    down_load.wait()
-    low = [low_part(p) for p in pieces]
-    for key in ((1, 0), (0, 1), (0, 0)):
-        crossing[key] = far(*key)
+    crossing[1, 0] = far(1, 0)
+    low = [low_second(p, low[p]) for p in pieces]
     early = near(1, 1, crossing[1, 1])
-    low = [low_second(p, low[p]) for p in pieces]
-    late = [None] * PIECES
+    crossing[0, 1] = far(0, 1)
+    crossing[0, 0] = far(0, 0)
+    low = [low_third(p, low[p]) for p in pieces]
     late[0] = near(1, 0, crossing[1, 0])[0]
     late[1] = near(0, 1, crossing[0, 1])[1]
-    low = [low_third(p, low[p]) for p in pieces]
     near(0, 0, crossing[0, 0])
+    low = [low_last(p, low[p]) for p in pieces]
     turned = [along_second(p, early[p]) for p in pieces]
-    low = [low_last(p, low[p]) for p in pieces]
     for p in pieces:
         keep_second(p, late[p])
     last = [along_z(p, 0, turned[p][0]) for p in pieces]

time: 32.6 us -> 31.4 us (0.963)
  Pallas kernels: 31 us -> 29.8 us
    pallas_call x1, Pallas kernels: 31 us -> 29.8 us  [body(): pl.pallas_call(kernel, out_shape=jax.ShapeDtypeStruct((width, rows), BF16...]
where the time goes in v3:
time: 31.4 us; the launch traced here: 31.2 us
  Pallas kernels  29.8 us (95%)
  local copies, waits for them, and re-layouts  1.47 us (5%)
    pallas_call x1, Pallas kernels, body(): pl.pallas_call(kernel, out_shape=jax.ShapeDtypeStruct((width, rows), BF16...  29.8 us
    unnamed x1, local copies, waits for them, and re-layouts  1.47 us

profile of v3, /device:TPU:0, one launch (start us, length us, event | category | flops | bytes accessed | tf_op | source)
XLA Modules:
  0.0 31.2 jit_solution(6429942439852331733)
XLA Ops:
  0.0 29.8 %shard_map.73 = bf16[256,128]{1,0:T(8,128)(2,1)} custom-call(bf16[128,256]{1,0:T(8,128)(2,1)} %q_hbm.1, s32[1,128]{1,0:T(1,128)} %bitcast.4, s32[1,128]{1,0:T(1,128)} %bitcast.5, bf16[1,128,128,256]{3,2,1,0:T(8,128)(2,1)} %cache_hbm.1, bf16[256,8192]{1,0:T(8,128)(2,1)} %w_hbm.1, bf16[8,64,256]{2,1,0:T(8,128)(2,1)} %bitcast.3, bf16[8,64,256]{2,1,0:T(8,128)(2,1)} %up_hbm), custom_call_target="tpu_custom_call" | custom-call | tf_op jit(solution)/shard_map/pallas_call | solution.py:319
  29.8 1.5 %copy.9 = bf16[256,128]{1,0:T(8,128)(2,1)} copy(bf16[256,128]{1,0:T(8,128)(2,1)} %shard_map.73) | data formatting | bytes 131072

commit v4 on v3

--- a/solution.py
+++ b/solution.py
@@ -53,7 +53,15 @@
     ]
     down_load = pltpu.make_async_copy(down_hbm, down, load_sem.at[chunks])
     up_load = pltpu.make_async_copy(up_hbm, up, load_sem.at[chunks + 1])
-    w_load = pltpu.make_async_copy(w_hbm, w, load_sem.at[chunks + 2])
+    quarter = w.shape[0] // 4
+    w_loads = [
+        pltpu.make_async_copy(
+            w_hbm.at[pl.ds(i * quarter, quarter)],
+            w.at[pl.ds(i * quarter, quarter)],
+            load_sem.at[chunks + (2, 6, 7, 8)[i]],
+        )
+        for i in range(4)
+    ]
     small_loads = [
         pltpu.make_async_copy(src, dst, load_sem.at[chunks + 3 + i])
         for i, (src, dst) in enumerate(((q_hbm, q_ref), (len_hbm, len_ref), (idx_hbm, idx_ref)))
@@ -62,10 +70,11 @@
         load.start()
     for c in range(chunks // 2):
         cache_loads[c].start()
-    down_load.start()
-    w_load.start()
     for c in range(chunks // 2, chunks):
         cache_loads[c].start()
+    down_load.start()
+    for load in w_loads:
+        load.start()
     up_load.start()
 
     barrier = pltpu.get_barrier_semaphore()
@@ -255,11 +264,12 @@
         return total
 
     pieces = range(PIECES)
-    lax.fori_loop(0, chunks, attend, 0)
+    lax.fori_loop(0, chunks, attend, 0, unroll=2)
     pl.semaphore_wait(barrier, len(peers))
     down_load.wait()
     low = [low_part(p) for p in pieces]
-    w_load.wait()
+    for load in w_loads:
+        load.wait()
     crossing = {}
     late = [None] * PIECES
     crossing[1, 1] = far(1, 1)
@@ -339,7 +349,7 @@
             pltpu.VMEM(low, F32), pltpu.VMEM(low, F32), pltpu.VMEM(low, F32), pltpu.VMEM(low, F32),
             pltpu.VMEM(low, F32), pltpu.VMEM(low, F32), pltpu.VMEM(low, F32),
             pltpu.VMEM((PIECES, 3) + low[1:], F32),
-            pltpu.SemaphoreType.DMA((chunks + 6,)),
+            pltpu.SemaphoreType.DMA((chunks + 9,)),
             pltpu.SemaphoreType.DMA((PIECES, 17)),
             pltpu.SemaphoreType.DMA((PIECES, 17)),
         ],

time: 31.4 us -> 31.3 us (level)
  no operation moved by 1% of the time
where the time goes in v4:
time: 31.3 us; the launch traced here: 31.1 us
  Pallas kernels  29.6 us (95%)
  local copies, waits for them, and re-layouts  1.47 us (5%)
    pallas_call x1, Pallas kernels, body(): pl.pallas_call(kernel, out_shape=jax.ShapeDtypeStruct((width, rows), BF16...  29.6 us
    unnamed x1, local copies, waits for them, and re-layouts  1.47 us

profile of v4, /device:TPU:0, one launch (start us, length us, event | category | flops | bytes accessed | tf_op | source)
XLA Modules:
  0.0 31.1 jit_solution(14047575260500705582)
XLA Ops:
  0.0 29.6 %shard_map.73 = bf16[256,128]{1,0:T(8,128)(2,1)} custom-call(bf16[128,256]{1,0:T(8,128)(2,1)} %q_hbm.1, s32[1,128]{1,0:T(1,128)} %bitcast.4, s32[1,128]{1,0:T(1,128)} %bitcast.5, bf16[1,128,128,256]{3,2,1,0:T(8,128)(2,1)} %cache_hbm.1, bf16[256,8192]{1,0:T(8,128)(2,1)} %w_hbm.1, bf16[8,64,256]{2,1,0:T(8,128)(2,1)} %bitcast.3, bf16[8,64,256]{2,1,0:T(8,128)(2,1)} %up_hbm), custom_call_target="tpu_custom_call" | custom-call | tf_op jit(solution)/shard_map/pallas_call | solution.py:329
  29.7 1.5 %copy.9 = bf16[256,128]{1,0:T(8,128)(2,1)} copy(bf16[256,128]{1,0:T(8,128)(2,1)} %shard_map.73) | data formatting | bytes 131072
